TPU v7x, 256 devices: a whole 4x4x8 slice. The times are simulated.
256 devices in a mesh: row: 16 (over z, x_lo), col: 16 (over y, x_hi, core).
Axes of the slice: x: 4 (x_hi: 2, x_lo: 2; x = x_hi * 2 + x_lo), y: 4, z: 8, core: 2. Of those that a mesh axis runs over, the one named last changes fastest.
Arguments:
- object_slices: float32 [2, 4, 4096, 4096], P(None, None, 'row', 'col'), may hold values from -1 to 1
- positions: int32 [16, 16, 2, 2], P('row', 'col'), may hold values from 0 to 128
- intensities: float32 [16, 16, 2, 256, 256], P('row', 'col'), may hold values from 0 to 0.8
- probe: float32 [2, 256, 256], replicated, may hold values from -6 to 6
- propagator: float32 [256, 256], replicated, may hold values from -3.140625 to 3.140625
Outputs:
- gradient: float32 [2, 4, 4096, 4096], P(None, None, 'row', 'col')
- updated: float32 [2, 4, 4096, 4096], P(None, None, 'row', 'col')
Inputs may be any that keep to these rules, and one draw needn't show every extreme that they name: `positions`: each probe window lies inside its tile widened by 64 pixels on every side.
All inputs are finite; a program needn't handle non-finite values.
Results may differ from a plain program's by a relative error of at most 0.0003.
Values sent between devices are 32-bit elements; how exact they have to be, the bound alone decides.
No kernel may reach another device: no remote copies, remote signals or barrier semaphores. Data moves between devices by JAX's collectives and lax.ppermute only.
A program may use at most 128 MiB of HBM per device.

v0:
```python
import functools

import jax
import jax.numpy as jnp
import ml_dtypes
import numpy as np
from jax import lax
from jax.experimental import pallas as pl
from jax.experimental.pallas import tpu as pltpu
from jax.sharding import PartitionSpec as P

HALO = 64
W = 256
HALF = 128
F32 = jnp.float32
BF16 = jnp.bfloat16
AXES = ("row", "col")
RATE = 0.5
PARTED = 2


def fourier_tables():
    n = np.arange(HALF)
    angle = 2.0 * np.pi * (np.outer(n, n) % HALF) / HALF
    cos, sin = np.cos(angle) / 16.0, np.sin(angle) / 16.0
    forward = np.block([[cos, sin], [-sin, cos]]).astype(np.float32)
    both = []
    for matrix in (forward, forward.T):
        high = matrix.astype(ml_dtypes.bfloat16)
        low = (matrix - high.astype(np.float32)).astype(ml_dtypes.bfloat16)
        both += [high, low]
    matrices = np.stack(both)
    turn = 2.0 * np.pi * n / W
    twiddle = np.stack([np.cos(turn), np.sin(turn)]).astype(np.float32)
    by_row = np.broadcast_to(twiddle[:, :, None], (2, HALF, HALF)).copy()
    by_lane = np.broadcast_to(twiddle[:, None, :], (2, 8, HALF)).copy()
    order = np.zeros((W, W), np.float32)
    order[2 * n, n] = 1.0
    order[2 * n + 1, HALF + n] = 1.0
    return matrices, by_row, by_lane, np.stack([order.T, order]).astype(ml_dtypes.bfloat16)


def lanes(rows):
    return lax.broadcasted_iota(jnp.int32, (rows, HALF), 1)


def rows_of(first, rows):
    return first + lax.broadcasted_iota(jnp.int32, (rows, HALF), 0)


def swap(x):
    return pltpu.roll(x, HALO, 1)


def split(x):
    high = x.astype(BF16)
    return high, (x - high.astype(F32)).astype(BF16)


def mul(ar, ai, br, bi):
    return ar * br - ai * bi, ar * bi + ai * br


def mul_conj(ar, ai, br, bi):
    return ar * br + ai * bi, ar * bi - ai * br


def dot(a, b):
    return jnp.dot(a, b, preferred_element_type=F32)


def pack_left(re0, im0):
    low = lanes(re0.shape[0]) < HALO
    return jnp.where(low, re0, swap(im0))


def pack_right(re1, im1):
    low = lanes(re1.shape[0]) < HALO
    return jnp.where(low, swap(im1), re1)


def pack_kernel(core_ref, object_ref, top, bottom, out_first, out_last, out_top, out_bottom, in_rows):
    core = core_ref[0]
    for s in range(4):
        for c in range(2):
            top[c, s] = object_ref[c, s, :HALO, :]
            bottom[c, s] = object_ref[c, s, W - HALO :, :]
        for r in range(0, W, 64):
            re, im = object_ref[0, s, r : r + 64, :], object_ref[1, s, r : r + 64, :]
            left = pack_left(re[:, :HALF], im[:, :HALF])
            right = pack_right(re[:, HALF:], im[:, HALF:])
            packed = jnp.where(core == 1, right, left)
            in_rows[s, r : r + 64, :] = jnp.where(core == 1, left, right)
            if s < PARTED:
                out_first[s, r : r + 64, :] = packed
            else:
                out_last[s - PARTED, r : r + 64, :] = packed
            if r == 0:
                out_top[s] = packed
            if r == W - HALO:
                out_bottom[s] = packed


def relay_kernel(core_ref, below_ref, above_ref, last_ref, first_ref, corner_below, corner_above, measured, inward, last):
    core = core_ref[0]
    last[...] = last_ref[...]
    for s in range(4):
        for at, ref in ((0, below_ref), (HALO, above_ref)):
            re, im = ref[0, s], ref[1, s]
            left = pack_left(re[:, :HALF], im[:, :HALF])
            right = pack_right(re[:, HALF:], im[:, HALF:])
            inward[s, at : at + HALO, :] = jnp.where(core == 1, left, right)


def prepare(pos_ref, probe_ref, propagator_ref, intensity_ref, order_ref, wave_ref, phase_ref, measured_ref):
    for k in range(2):
        a = lax.rem(pos_ref[k, 0] + (W - HALO), W)
        b = lax.rem(pos_ref[k, 1] + (W - HALO), W)
        for c in range(2):
            wave_ref[0, k, c] = pltpu.roll(pltpu.roll(probe_ref[c], a, 0), b, 1)

    def ordered(x):
        for left in (True, False):
            total = None
            for _ in range(3):
                part = x.astype(BF16)
                x = x - part.astype(F32)
                term = dot(order_ref[0], part) if left else dot(part, order_ref[1])
                total = term if total is None else total + term
            x = total
        return x

    angle = ordered(propagator_ref[...])
    phase_ref[0] = jnp.cos(angle)
    phase_ref[1] = jnp.sin(angle)
    for k in range(2):
        measured_ref[k] = ordered(intensity_ref[k])


STEP = 32


class Transform:
    def __init__(self, tables, scratch):
        self.matrices, self.by_row, self.by_lane = tables
        self.xr_h, self.xr_l, self.xl_h, self.xl_l, self.wr, self.wl = scratch

    def put_rows(self, k, e, r, re, im):
        cols = slice(e * W, (e + 1) * W)
        n = re.shape[0]
        for base, x in ((0, re), (HALF, im)):
            high, low = split(x)
            self.xr_h[k, base + r : base + r + n, cols] = high
            self.xr_l[k, base + r : base + r + n, cols] = low

    def put_lanes(self, k, e, r, re, im):
        n = re.shape[0]
        for base, x in ((0, re), (HALF, im)):
            high, low = split(x)
            self.xl_h[k, e * W + r : e * W + r + n, base : base + HALF] = high
            self.xl_l[k, e * W + r : e * W + r + n, base : base + HALF] = low

    def enter(self, k, r, n, first, second):
        c = jnp.concatenate([self.by_row[0, r : r + n, :]] * 2, axis=1)
        s = jnp.concatenate([self.by_row[1, r : r + n, :]] * 2, axis=1)
        self.put_rows(k, 0, r, first[0] + second[0], first[1] + second[1])
        dr, di = first[0] - second[0], first[1] - second[1]
        self.put_rows(k, 1, r, dr * c + di * s, di * c - dr * s)

    def dot_rows(self, k, inverse):
        high, low = self.matrices[2 * inverse], self.matrices[2 * inverse + 1]
        for cols in (slice(0, W), slice(W, 2 * W)):
            xh, xl = self.xr_h[k, :, cols], self.xr_l[k, :, cols]
            self.wr[k, :, cols] = dot(high, xh) + dot(high, xl) + dot(low, xh)

    def dot_lanes(self, k, inverse):
        high, low = self.matrices[2 - 2 * inverse], self.matrices[3 - 2 * inverse]
        for rows in (slice(0, W), slice(W, 2 * W)):
            xh, xl = self.xl_h[k, rows], self.xl_l[k, rows]
            self.wl[k, rows] = dot(xh, high) + dot(xl, high) + dot(xh, low)

    def along_lanes(self, k):
        for e in range(2):
            cols = slice(e * W, (e + 1) * W)
            for r in range(0, HALF, STEP):
                n = STEP
                re = self.wr[k, r : r + n, cols]
                im = self.wr[k, HALF + r : HALF + r + n, cols]
                row = e * HALF + r
                c = jnp.concatenate([self.by_lane[0]] * (n // 8), axis=0)
                s = jnp.concatenate([self.by_lane[1]] * (n // 8), axis=0)
                re0, re1, im0, im1 = re[:, :HALF], re[:, HALF:], im[:, :HALF], im[:, HALF:]
                self.put_lanes(k, 0, row, re0 + re1, im0 + im1)
                dr, di = re0 - re1, im0 - im1
                self.put_lanes(k, 1, row, dr * c + di * s, di * c - dr * s)

    def modify(self, k, change):
        for e in range(2):
            for r in range(0, W, STEP):
                n = STEP
                rows = slice(e * W + r, e * W + r + n)
                re, im = change(e, slice(r, r + n), self.wl[k, rows, :HALF], self.wl[k, rows, HALF:])
                self.put_lanes(k, e, r, re, im)

    def back_along_lanes(self, k):
        for e in range(2):
            for r in range(0, HALF, STEP):
                n = STEP
                row = e * HALF + r
                c = jnp.concatenate([self.by_lane[0]] * (n // 8), axis=0)
                s = jnp.concatenate([self.by_lane[1]] * (n // 8), axis=0)
                er, ei = self.wl[k, row : row + n, :HALF], self.wl[k, row : row + n, HALF:]
                tr, ti = self.wl[k, W + row : W + row + n, :HALF], self.wl[k, W + row : W + row + n, HALF:]
                tr, ti = tr * c - ti * s, ti * c + tr * s
                re = jnp.concatenate([er + tr, er - tr], axis=1)
                im = jnp.concatenate([ei + ti, ei - ti], axis=1)
                self.put_rows(k, e, r, re, im)

    def around(self, entering, changes):
        for k in range(2):
            entering(k)
            self.dot_rows(k, 0)
        for k in range(2):
            self.along_lanes(k)
            self.dot_lanes(k, 0)
        for k in range(2):
            self.modify(k, changes[k])
            self.dot_lanes(k, 1)
        for k in range(2):
            self.back_along_lanes(k)
            self.dot_rows(k, 1)

    def leave(self, k, r, n):
        c = jnp.concatenate([self.by_row[0, r : r + n, :]] * 2, axis=1)
        s = jnp.concatenate([self.by_row[1, r : r + n, :]] * 2, axis=1)
        er, ei = self.wr[k, r : r + n, :W], self.wr[k, HALF + r : HALF + r + n, :W]
        tr, ti = self.wr[k, r : r + n, W:], self.wr[k, HALF + r : HALF + r + n, W:]
        tr, ti = tr * c - ti * s, ti * c + tr * s
        return (er + tr, ei + ti), (er - tr, ei - ti)


def phase_of(phase_ref, sign):
    def change(e, rows, re, im):
        cols = slice(e * HALF, (e + 1) * HALF)
        pr, pi = phase_ref[0, rows, cols], phase_ref[1, rows, cols]
        return mul(re, im, pr, pi) if sign > 0 else mul_conj(pr, pi, re, im)

    return change


def misfit_of(measured_ref, k):
    def change(e, rows, re, im):
        cols = slice(e * HALF, (e + 1) * HALF)
        misfit = re * re + im * im - measured_ref[k, rows, cols]
        return misfit * re, misfit * im

    return change


class Windows:
    def __init__(self, pos_ref, core_ref, refs, side, at):
        self.at = at
        self.core = core_ref[0]
        self.object, self.below, self.above, self.out, self.out_below, self.out_above, self.inner, self.in_rows = refs
        self.side = side
        self.shift = [(pos_ref[k, 0] - HALO, pos_ref[k, 1] - HALO) for k in range(2)]

    def gather_sides(self, s):
        for r in range(0, 384, 64):
            if r < W:
                outer = self.out[s - self.at, r : r + 64]
            else:
                outer = (self.out_below if r == W else self.out_above)[s]
            inner = self.in_rows[s, r : r + 64] if r < W else self.inner[s, r - W : r - W + 64]
            right = jnp.where(self.core == 1, outer, inner)
            left = jnp.where(self.core == 1, inner, outer)
            low = lanes(64) < HALO
            self.side[0, r : r + 64] = jnp.where(low, right, left)
            self.side[1, r : r + 64] = swap(jnp.where(low, left, right))

    def with_sides(self, k, own, side):
        b = self.shift[k][1]
        lane = lanes(own.shape[0])
        return (
            jnp.where(lane < b, side, own[:, :HALF]),
            jnp.where(lane >= HALF + b, side, own[:, HALF:]),
        )

    def window(self, s, k, c, r, n):
        tiles = self.with_sides(k, self.object[c, s, r : r + n, :], self.side[c, r : r + n])
        a = self.shift[k][0]
        if r < HALO:
            other = self.with_sides(k, self.below[c, s, r : r + n, :], self.side[c, W + r : W + r + n])
            wraps = rows_of(r, n) < a
        elif r >= W - HALO:
            q = r - (W - HALO)
            other = self.with_sides(k, self.above[c, s, q : q + n, :], self.side[c, W + HALO + q : W + HALO + q + n])
            wraps = rows_of(r, n) >= W + a
        else:
            return jnp.concatenate(tiles, axis=1)
        return jnp.concatenate([jnp.where(wraps, o, t) for t, o in zip(tiles, other)], axis=1)


class Folding:
    def __init__(self, pos_ref, core_ref, refs, at):
        self.at = at
        self.core = core_ref[0]
        self.own, self.below, self.above, self.out, self.out_below, self.out_above, self.inner = refs
        self.shift = [(pos_ref[k, 0] - HALO, pos_ref[k, 1] - HALO) for k in range(2)]

    def part(self, terms, keep):
        n = terms[0].shape[0]
        lane = lanes(n)
        tiles, sides = [0.0, 0.0], 0.0
        for k, term in enumerate(terms):
            b = self.shift[k][1]
            zero = jnp.zeros((n, HALF), F32)
            for t, wraps in enumerate((lane < b, lane >= HALF + b)):
                x = term[:, t * HALF : (t + 1) * HALF]
                if keep is not None:
                    x = jnp.where(keep[k], x, zero)
                tiles[t] = tiles[t] + jnp.where(wraps, zero, x)
                sides = sides + jnp.where(wraps, x, zero)
        return jnp.concatenate(tiles, axis=1), sides

    def sides_to(self, j, r, n, re, im, out):
        low = lanes(n) < HALO
        flipped = swap(im)
        right = jnp.where(low, re, flipped)
        left = jnp.where(low, flipped, re)
        ref, i, at = out
        ref[i, at : at + n] = jnp.where(self.core == 1, right, left)
        self.inner[j, r : r + n] = jnp.where(self.core == 1, left, right)

    def put(self, j, r, terms):
        n = terms[0][0].shape[0]
        if HALO <= r < W - HALO:
            parts = [self.part(terms[c], None) for c in range(2)]
        else:
            row = rows_of(r, n)
            if r < HALO:
                wraps = [row < self.shift[k][0] for k in range(2)]
                band, out, at, q = self.below, self.out_below, r, W + r
            else:
                wraps = [row >= W + self.shift[k][0] for k in range(2)]
                at = r - (W - HALO)
                band, out, q = self.above, self.out_above, W + HALO + at
            away = [self.part(terms[c], wraps) for c in range(2)]
            for c in range(2):
                band[c, j, at : at + n, :] = away[c][0]
            self.sides_to(j, q, n, away[0][1], away[1][1], (out, j, at))
            stays = [jnp.logical_not(w) for w in wraps]
            parts = [self.part(terms[c], stays) for c in range(2)]
        for c in range(2):
            self.own[c, j, r : r + n, :] = parts[c][0]
        self.sides_to(j, r, n, parts[0][1], parts[1][1], (self.out, j - self.at, r))


PAIRS = [(r, STEP) for r in range(0, HALF, STEP)]


def forward_slices(t, w, waves, seen, phase, low, high):
    def slice_step(s, carry):
        w.gather_sides(s)

        def entering(k):
            for r, n in PAIRS:
                exits = []
                for q in (r, r + HALF):
                    o = [w.window(s, k, c, q, n) for c in range(2)]
                    for c in range(2):
                        seen[s, k, c, q : q + n, :] = o[c]
                    exits.append(mul(waves[s, k, 0, q : q + n, :], waves[s, k, 1, q : q + n, :], *o))
                t.enter(k, r, n, *exits)

        t.around(entering, [phase_of(phase, 1)] * 2)
        for k in range(2):
            for r, n in PAIRS:
                for q, pair in zip((r, r + HALF), t.leave(k, r, n)):
                    for c in range(2):
                        waves[s + 1, k, c, q : q + n, :] = pair[c]
        return carry

    lax.fori_loop(low, high, slice_step, 0)


def collect(t, f, waves, seen, back, s):
    for r, n in PAIRS:
        pairs = [t.leave(k, r, n) for k in range(2)]
        for half, q in enumerate((r, r + HALF)):
            terms = [[], []]
            for k in range(2):
                g = pairs[k][half]
                wave = waves[s, k, 0, q : q + n, :], waves[s, k, 1, q : q + n, :]
                for c, x in enumerate(mul_conj(*wave, *g)):
                    terms[c].append(x)
                o = seen[s, k, 0, q : q + n, :], seen[s, k, 1, q : q + n, :]
                back[k, 0, q : q + n, :], back[k, 1, q : q + n, :] = mul_conj(*o, *g)
            f.put(s, q, terms)


def backward_slices(t, f, waves, seen, phase, back, high, low):
    def slice_step(i, carry):
        s = high - 1 - i

        def entering(k):
            for r, n in PAIRS:
                t.enter(k, r, n, *[(back[k, 0, q : q + n, :], back[k, 1, q : q + n, :]) for q in (r, r + HALF)])

        t.around(entering, [phase_of(phase, -1)] * 2)
        collect(t, f, waves, seen, back, s)
        return carry

    lax.fori_loop(0, high - low, slice_step, 0)


def forward_kernel(pos, core, waves_in, phase, obj, below, above, out, out_below, out_above, inner, in_rows,
                   mats, by_row, by_lane, waves, seen, xr_h, xr_l, xl_h, xl_l, wr, wl, side):
    t = Transform((mats, by_row, by_lane), (xr_h, xr_l, xl_h, xl_l, wr, wl))
    w = Windows(pos, core, (obj, below, above, out, out_below, out_above, inner, in_rows), side, 0)
    forward_slices(t, w, waves, seen, phase, 0, PARTED)


def turn_kernel(pos, core, waves_in, seen_in, phase, measured, obj, below, above, out, out_below, out_above, inner,
                in_rows, mats, by_row, by_lane,
                waves, seen, back, own, g_below, g_above, g_out_below, g_out_above, g_inner, g_out,
                xr_h, xr_l, xl_h, xl_l, wr, wl, side):
    t = Transform((mats, by_row, by_lane), (xr_h, xr_l, xl_h, xl_l, wr, wl))
    w = Windows(pos, core, (obj, below, above, out, out_below, out_above, inner, in_rows), side, PARTED)
    f = Folding(pos, core, (own, g_below, g_above, g_out, g_out_below, g_out_above, g_inner), PARTED)
    forward_slices(t, w, waves, seen, phase, PARTED, 3)
    w.gather_sides(3)

    def entering(k):
        for r, n in PAIRS:
            exits = []
            for q in (r, r + HALF):
                o = [w.window(3, k, c, q, n) for c in range(2)]
                for c in range(2):
                    seen[3, k, c, q : q + n, :] = o[c]
                exits.append(mul(waves[3, k, 0, q : q + n, :], waves[3, k, 1, q : q + n, :], *o))
            t.enter(k, r, n, *exits)

    t.around(entering, [misfit_of(measured, k) for k in range(2)])
    collect(t, f, waves, seen, back, 3)
    backward_slices(t, f, waves, seen, phase, back, 3, PARTED)


def backward_kernel(pos, core, back_in, waves, seen, phase, own_in, g_below_in, g_above_in, g_out_below_in, g_out_above_in,
                    g_inner_in, mats, by_row, by_lane,
                    back, own, g_below, g_above, g_out_below, g_out_above, g_inner, g_out,
                    xr_h, xr_l, xl_h, xl_l, wr, wl):
    t = Transform((mats, by_row, by_lane), (xr_h, xr_l, xl_h, xl_l, wr, wl))
    f = Folding(pos, core, (own, g_below, g_above, g_out, g_out_below, g_out_above, g_inner), 0)
    backward_slices(t, f, waves, seen, phase, back, PARTED, 0)


def spread(core, outer, inner):
    low = lanes(outer.shape[0]) < HALO
    zero = jnp.zeros(outer.shape, F32)
    left = jnp.where(core == 1, inner, outer)
    right = jnp.where(core == 1, outer, inner)
    left_im, right_im = swap(left), swap(right)
    re = jnp.concatenate([jnp.where(low, left, zero), jnp.where(low, zero, right)], axis=1)
    im = jnp.concatenate([jnp.where(low, left_im, zero), jnp.where(low, zero, right_im)], axis=1)
    return re, im


def bands_kernel(core_ref, g_below, g_above, inner, out_last, to_below, to_above):
    core = core_ref[0]
    for s in range(4):
        for at, source, target in ((W, g_below, to_below), (W + HALO, g_above, to_above)):
            part = inner[s, at : at + HALO]
            more = spread(core, jnp.zeros_like(part), part)
            for c in range(2):
                target[c, s] = source[c, s] + more[c]


def final_kernel(core_ref, obj, own, from_above, from_below, out_first, out_last, out_above, out_below, inner,
                 gradient_out, updated_out, gradient, updated, sent):
    core = core_ref[0]
    copies = []
    for s in range(4):
        out, j = (out_first, s) if s < PARTED else (out_last, s - PARTED)
        for r in range(0, W, 64):
            side = out[j, r : r + 64]
            if r == 0:
                side = side + out_above[s]
            if r == W - HALO:
                side = side + out_below[s]
            more = spread(core, side, inner[s, r : r + 64])
            for c in range(2):
                total = own[c, s, r : r + 64, :] + more[c]
                if r == 0:
                    total = total + from_above[c, s]
                if r == W - HALO:
                    total = total + from_below[c, s]
                gradient[s, c, r : r + 64, :] = total
                updated[s, c, r : r + 64, :] = obj[c, s, r : r + 64, :] - RATE * total
        for i, (held, target) in enumerate(((gradient, gradient_out), (updated, updated_out))):
            copies.append(pltpu.make_async_copy(held.at[s], target.at[:, s], sent.at[2 * s + i]))
            copies[-1].start()
    for copy in copies:
        copy.wait()


SMEM = pl.BlockSpec(memory_space=pltpu.SMEM)
VMEM = pl.BlockSpec(memory_space=pltpu.VMEM)
ANYWHERE = pl.BlockSpec(memory_space=pl.ANY)
HBM = pl.BlockSpec(memory_space=pltpu.HBM)


def call(kernel, outs, args, scalars, scratch=(), flops=0, moved=2**20, limit=24, aliases=None, places=None, targets=None):
    shapes = [jax.ShapeDtypeStruct(shape, F32) for shape in outs]
    return pl.pallas_call(
        kernel,
        out_shape=shapes,
        in_specs=[SMEM] * scalars + (places or [VMEM] * (len(args) - scalars)),
        out_specs=targets or [VMEM] * len(shapes),
        scratch_shapes=list(scratch),
        input_output_aliases=aliases or {},
        compiler_params=pltpu.CompilerParams(vmem_limit_bytes=limit * 1024 * 1024),
        cost_estimate=pl.CostEstimate(flops=flops, bytes_accessed=moved, transcendentals=0),
    )(*args)


TRANSFORM_SCRATCH = [
    pltpu.VMEM((2, W, 2 * W), BF16),
    pltpu.VMEM((2, W, 2 * W), BF16),
    pltpu.VMEM((2, 2 * W, W), BF16),
    pltpu.VMEM((2, 2 * W, W), BF16),
    pltpu.VMEM((2, W, 2 * W), F32),
    pltpu.VMEM((2, 2 * W, W), F32),
]
SIDE_SCRATCH = pltpu.VMEM((2, 384, HALF), F32)
STACK = (4, 2, 2, W, W)


def routes(rows, cols):
    def out(c):
        return c + 1 if c % 2 else c - 1

    def build(step, col):
        return [
            (r * cols + c, (r + step) % rows * cols + col(c) % cols) for r in range(rows) for c in range(cols)
        ]

    return {
        "up": build(-1, lambda c: c),
        "down": build(1, lambda c: c),
        "out": build(0, out),
        "out_up": build(-1, out),
        "out_down": build(1, out),
        "in": build(0, lambda c: c - 1 if c % 2 else c + 1),
    }


def on_device(obj, positions, intensities, probe, propagator, *, route):
    matrices, by_row, by_lane, order = (jnp.asarray(x) for x in fourier_tables())
    tables = (matrices, by_row, by_lane)
    core = (lax.axis_index("col") % 2).astype(jnp.int32).reshape(1)
    pos = positions[0, 0]
    flops = 2 * 2 * 8 * 3 * 2 * W**3 // 2
    bands, corners, columns, both = (2, 4, HALO, W), (4, HALO, HALF), (4, W, HALF), (4, 2 * HALO, HALF)
    first, last = (PARTED, W, HALF), (4 - PARTED, W, HALF)

    def send(x, way):
        return lax.ppermute(x, AXES, route[way])

    top, bottom, out_first, out_last, out_top, out_bottom, in_rows = call(
        pack_kernel, [bands, bands, first, last, corners, corners, columns], (core, obj), 1
    )
    waves, phase, measured = call(
        prepare,
        [STACK, (2, W, W), (2, W, W)],
        (pos, probe, propagator, intensities[0, 0], order),
        1,
    )
    in_rows, out_bottom = lax.optimization_barrier((send(in_rows, "in"), out_bottom))
    below, above = send(top, "up"), send(bottom, "down")
    out_first = send(out_first, "out")
    corner_below, corner_above = send(out_top, "out_up"), send(out_bottom, "out_down")
    inward, out_last = call(
        relay_kernel,
        [both, last],
        (core, below, above, out_last, out_first, corner_below, corner_above, measured),
        1,
        places=[VMEM] * 3 + [ANYWHERE] * 4,
    )
    out_last = send(out_last, "out")
    inner = send(inward, "in")

    waves, seen = call(
        forward_kernel,
        [STACK, STACK],
        (pos, core, waves, phase, obj, below, above, out_first, corner_below, corner_above, inner, in_rows, *tables),
        2,
        TRANSFORM_SCRATCH + [SIDE_SCRATCH],
        flops=PARTED * flops,
        aliases={2: 0},
    )
    sums = [(2, 4, W, W), bands, bands, corners, corners, (4, 384, HALF)]
    waves, seen, back, *terms, out_last = call(
        turn_kernel,
        [STACK, STACK, (2, 2, W, W), *sums, last],
        (pos, core, waves, seen, phase, measured, obj, below, above, out_last, corner_below, corner_above, inner, in_rows, *tables),
        2,
        TRANSFORM_SCRATCH + [SIDE_SCRATCH],
        flops=(7 - 2 * PARTED) * flops,
        aliases={2: 0, 3: 1},
    )
    out_last = send(out_last, "out")
    _, own, g_below, g_above, g_out_below, g_out_above, g_inner, out_first = call(
        backward_kernel,
        [(2, 2, W, W), *sums, first],
        (pos, core, back, waves, seen, phase, *terms, *tables),
        2,
        TRANSFORM_SCRATCH,
        flops=PARTED * flops,
        aliases={2: 0, **{6 + i: 1 + i for i in range(6)}},
    )

    g_inner, out_last = lax.optimization_barrier((g_inner, out_last))
    inner = send(g_inner, "in")
    out_first = send(out_first, "out")
    out_above = send(g_out_below, "out_down")
    out_below = send(g_out_above, "out_up")
    to_below, to_above = call(
        bands_kernel, [bands, bands], (core, g_below, g_above, inner, out_last), 1, places=[VMEM] * 3 + [ANYWHERE]
    )
    from_above = send(to_below, "down")
    from_below = send(to_above, "up")
    return tuple(
        call(
            final_kernel,
            [(2, 4, W, W)] * 2,
            (core, obj, own, from_above, from_below, out_first, out_last, out_above, out_below, inner),
            1,
            [pltpu.VMEM((4, 2, W, W), F32), pltpu.VMEM((4, 2, W, W), F32), pltpu.SemaphoreType.DMA((8,))],
            targets=[HBM] * 2,
        )
    )


def solution(mesh):
    route = routes(mesh.shape["row"], mesh.shape["col"])
    return jax.shard_map(
        functools.partial(on_device, route=route),
        mesh=mesh,
        in_specs=(
            P(None, None, "row", "col"),
            P("row", "col", None, None),
            P("row", "col", None, None, None),
            P(),
            P(),
        ),
        out_specs=(P(None, None, "row", "col"), P(None, None, "row", "col")),
        check_vma=False,
    )
```

profile of v0, /device:TPU:31, one launch (start us, length us, event | category | flops | bytes accessed | tf_op | source)
XLA Modules:
  0.0 103.6 jit_solution(4502435121454117711)
XLA Ops:
  0.7 1.6 %copy-done = f32[2,4,256,256]{3,2,1,0:T(8,128)S(1)} copy-done((f32[2,4,256,256]{3,2,1,0:T(8,128)S(1)}, f32[2,4,256,256]{3,2,1,0:T(8,128)}, u32[]{:S(2)}) %copy-start) | copy-done | bytes 2097176
  2.2 0.4 shard_map.105
  2.6 0.8 collective-permute-start.4
  3.4 0.6 collective-permute-start
  3.9 1.8 %collective-permute-start.1 = (f32[2,4,64,256]{3,2,1,0:T(8,128)S(1)}, f32[2,4,64,256]{3,2,1,0:T(8,128)S(1)}, u32[]{:S(2)}, u32[]{:S(2)}) collective-permute-start(f32[2,4,64,256]{3,2,1,0:T(8,128)S(1)} %get-tuple-element.42), channel_id=1, source_target_pairs={{0,16},{1,17},{2,18},{3,19},{4,20},{5,21},{6,22},{7,23},{8,24},{9,... | collective-permute-start | bytes 1572872 | tf_op jit(solution)/shard_map/ppermute | solution.py:568
  5.8 1.3 %collective-permute-start.2 = (f32[2,256,128]{2,1,0:T(8,128)S(1)}, f32[2,256,128]{2,1,0:T(8,128)S(1)}, u32[]{:S(2)}, u32[]{:S(2)}) collective-permute-start(f32[2,256,128]{2,1,0:T(8,128)S(1)} %get-tuple-element.43), channel_id=1, source_target_pairs={{0,15},{1,2},{2,1},{3,4},{4,3},{5,6},{6,5},{7,8},{8,7},{9,10},{10,... | collective-permute-start | bytes 786440 | tf_op jit(solution)/shard_map/ppermute | solution.py:568
  7.1 7.9 %collective-permute-start.3 = (f32[4,64,128]{2,1,0:T(8,128)S(1)}, f32[4,64,128]{2,1,0:T(8,128)S(1)}, u32[]{:S(2)}, u32[]{:S(2)}) collective-permute-start(f32[4,64,128]{2,1,0:T(8,128)S(1)} %get-tuple-element.44), channel_id=1, source_target_pairs={{0,255},{1,242},{2,241},{3,244},{4,243},{5,246},{6,245},{7,248},{8... | collective-permute-start | bytes 393224 | tf_op jit(solution)/shard_map/ppermute | solution.py:568
  14.9 1.0 %copy-done.3 = f32[2,256,256]{2,1,0:T(8,128)S(1)} copy-done((f32[2,256,256]{2,1,0:T(8,128)S(1)}, f32[2,256,256]{2,1,0:T(8,128)}, u32[]{:S(2)}) %copy-start.3) | copy-done | bytes 524312
  16.0 1.0 %copy-done.4 = f32[1,1,2,256,256]{4,3,2,1,0:T(8,128)S(1)} copy-done((f32[1,1,2,256,256]{4,3,2,1,0:T(8,128)S(1)}, f32[1,1,2,256,256]{4,3,2,1,0:T(8,128)}, u32[]{:S(2)}) %copy-start.4) | copy-done | bytes 524312
  17.0 0.9 copy-done.5
  18.0 0.9 copy-done.6
  18.9 0.7 copy-done.9
  19.6 2.6 %shard_map.104 = (f32[4,2,2,256,256]{4,3,2,1,0:T(8,128)S(1)}, f32[2,256,256]{2,1,0:T(8,128)S(1)}, f32[2,256,256]{2,1,0:T(8,128)S(1)}) custom-call(s32[2,2]{1,0:T(2,128)S(1)} %bitcast.4, f32[2,256,256]{2,1,0:T(8,128)S(1)} %copy-done.3, f32[256,256]{1,0:T(8,128)S(1)} %copy-done.5, f32[2,256,256]{2,1,0:T(8,128)S(1)} %bitcast.3, bf16[2,256,256]{2,1,0:T(8,128)(2,1)S(1)} %copy-done.6), custom_call_target="tpu_custom_call" | custom-call | bytes 1048576 | tf_op jit(solution)/shard_map/pallas_call | solution.py:515
  22.2 13.0 %collective-permute-done.2.first_ref.out = f32[2,256,128]{2,1,0:T(8,128)S(1)} collective-permute-done((f32[2,256,128]{2,1,0:T(8,128)S(1)}, f32[2,256,128]{2,1,0:T(8,128)S(1)}, u32[]{:S(2)}, u32[]{:S(2)}) %collective-permute-start.2) | collective-permute-done | bytes 262176 | tf_op jit(solution)/shard_map/ppermute | solution.py:568
  35.5 3.2 %collective-permute-start.7 = (f32[2,256,128]{2,1,0:T(8,128)S(1)}, f32[2,256,128]{2,1,0:T(8,128)S(1)}, u32[]{:S(2)}, u32[]{:S(2)}) collective-permute-start(f32[2,256,128]{2,1,0:T(8,128)S(1)} %get-tuple-element.54), channel_id=1, source_target_pairs={{0,15},{1,2},{2,1},{3,4},{4,3},{5,6},{6,5},{7,8},{8,7},{9,10},{10,... | collective-permute-start | bytes 786440 | tf_op jit(solution)/shard_map/ppermute | solution.py:568
  38.8 0.9 copy-done.7
  39.7 5.1 %shard_map.107 = (f32[4,2,2,256,256]{4,3,2,1,0:T(8,128)S(1)}, f32[4,2,2,256,256]{4,3,2,1,0:T(8,128)S(1)}) custom-call(s32[2,2]{1,0:T(2,128)S(1)} %bitcast.5, s32[1]{0:T(128)} %bitcast.core_ref.core, f32[4,2,2,256,256]{4,3,2,1,0:T(8,128)S(1)} %get-tuple-element.39.waves_in, ...), custom_call_target="tpu_custom_call", output_to_operand_aliasing={{0}: (2, {})} | custom-call | flops 3221225472 | bytes 1048576 | tf_op jit(solution)/shard_map/pallas_call | solution.py:515
  44.8 0.6 collective-permute-done.7.out
  45.4 7.4 %shard_map.108 = (f32[4,2,2,256,256]{4,3,2,1,0:T(8,128)S(1)}, f32[4,2,2,256,256]{4,3,2,1,0:T(8,128)S(1)}, f32[2,2,256,256]{3,2,1,0:T(8,128)S(1)}, f32[2,4,256,25...) custom-call(s32[2,2]{1,0:T(2,128)S(1)} %bitcast.6, ...), custom_call_target="tpu_custom_call", output_to_operand_aliasing={{0}: (2, {}), {1}: (3, {})} | custom-call | flops 4831838208 | bytes 1048576 | tf_op jit(solution)/shard_map/pallas_call | solution.py:515
  52.9 4.1 %collective-permute-start.8 = (f32[2,256,128]{2,1,0:T(8,128)S(1)}, f32[2,256,128]{2,1,0:T(8,128)S(1)}, u32[]{:S(2)}, u32[]{:S(2)}) collective-permute-start(f32[2,256,128]{2,1,0:T(8,128)S(1)} %get-tuple-element.68), channel_id=1, source_target_pairs={{0,15},{1,2},{2,1},{3,4},{4,3},{5,6},{6,5},{7,8},{8,7},{9,10},{10,... | collective-permute-start | bytes 786440 | tf_op jit(solution)/shard_map/ppermute | solution.py:568
  57.0 5.3 %shard_map.109 = (f32[2,2,256,256]{3,2,1,0:T(8,128)S(1)}, f32[2,4,256,256]{3,2,1,0:T(8,128)S(1)}, f32[2,4,64,256]{3,2,1,0:T(8,128)S(1)}, f32[2,4,64,256]{3,2,1,0...) custom-call(s32[2,2]{1,0:T(2,128)S(1)} %bitcast.7, ...), custom_call_target="tpu_custom_call", output_to_operand_aliasing={{0}: (2, {}), {1}: (6, {}), {2}: (7, {}), {3}: (8, {}), {4}... | custom-call | flops 3221225472 | bytes 1048576 | tf_op jit(solution)/shard_map/pallas_call | solution.py:515
  62.3 0.5 collective-permute-start.9
  62.9 2.0 %collective-permute-done.9.inner = f32[4,384,128]{2,1,0:T(8,128)S(1)} collective-permute-done((f32[4,384,128]{2,1,0:T(8,128)S(1)}, f32[4,384,128]{2,1,0:T(8,128)S(1)}, u32[]{:S(2)}, u32[]{:S(2)}) %collective-permute-start.9) | collective-permute-done | bytes 786464 | tf_op jit(solution)/shard_map/ppermute | solution.py:568
  64.8 0.2 shard_map.110
  65.1 3.0 %collective-permute-start.10 = (f32[2,4,64,256]{3,2,1,0:T(8,128)S(1)}, f32[2,4,64,256]{3,2,1,0:T(8,128)S(1)}, u32[]{:S(2)}, u32[]{:S(2)}) collective-permute-start(f32[2,4,64,256]{3,2,1,0:T(8,128)S(1)} %get-tuple-element.71), channel_id=1, source_target_pairs={{0,16},{1,17},{2,18},{3,19},{4,20},{5,21},{6,22},{7,23},{8,24},{9,... | collective-permute-start | bytes 1572872 | tf_op jit(solution)/shard_map/ppermute | solution.py:568
  68.0 4.7 %collective-permute-start.12 = (f32[2,256,128]{2,1,0:T(8,128)S(1)}, f32[2,256,128]{2,1,0:T(8,128)S(1)}, u32[]{:S(2)}, u32[]{:S(2)}) collective-permute-start(f32[2,256,128]{2,1,0:T(8,128)S(1)} %get-tuple-element.73), channel_id=1, source_target_pairs={{0,15},{1,2},{2,1},{3,4},{4,3},{5,6},{6,5},{7,8},{8,7},{9,10},{10,... | collective-permute-start | bytes 786440 | tf_op jit(solution)/shard_map/ppermute | solution.py:568
  72.7 2.5 %collective-permute-start.13 = (f32[4,64,128]{2,1,0:T(8,128)S(1)}, f32[4,64,128]{2,1,0:T(8,128)S(1)}, u32[]{:S(2)}, u32[]{:S(2)}) collective-permute-start(f32[4,64,128]{2,1,0:T(8,128)S(1)} %get-tuple-element.74), channel_id=1, source_target_pairs={{0,31},{1,18},{2,17},{3,20},{4,19},{5,22},{6,21},{7,24},{8,23},{9,... | collective-permute-start | bytes 393224 | tf_op jit(solution)/shard_map/ppermute | solution.py:568
  75.2 2.6 %collective-permute-start.14 = (f32[4,64,128]{2,1,0:T(8,128)S(1)}, f32[4,64,128]{2,1,0:T(8,128)S(1)}, u32[]{:S(2)}, u32[]{:S(2)}) collective-permute-start(f32[4,64,128]{2,1,0:T(8,128)S(1)} %get-tuple-element.75), channel_id=1, source_target_pairs={{0,255},{1,242},{2,241},{3,244},{4,243},{5,246},{6,245},{7,248},{8... | collective-permute-start | bytes 393224 | tf_op jit(solution)/shard_map/ppermute | solution.py:568
  77.8 4.3 %collective-permute-done.13.out_above = f32[4,64,128]{2,1,0:T(8,128)S(1)} collective-permute-done((f32[4,64,128]{2,1,0:T(8,128)S(1)}, f32[4,64,128]{2,1,0:T(8,128)S(1)}, u32[]{:S(2)}, u32[]{:S(2)}) %collective-permute-start.13) | collective-permute-done | bytes 131104 | tf_op jit(solution)/shard_map/ppermute | solution.py:568
  82.1 6.3 %collective-permute-done.14.out_below = f32[4,64,128]{2,1,0:T(8,128)S(1)} collective-permute-done((f32[4,64,128]{2,1,0:T(8,128)S(1)}, f32[4,64,128]{2,1,0:T(8,128)S(1)}, u32[]{:S(2)}, u32[]{:S(2)}) %collective-permute-start.14) | collective-permute-done | bytes 131104 | tf_op jit(solution)/shard_map/ppermute | solution.py:568
  88.4 12.8 %collective-permute-done.12.out_first = f32[2,256,128]{2,1,0:T(8,128)S(1)} collective-permute-done((f32[2,256,128]{2,1,0:T(8,128)S(1)}, f32[2,256,128]{2,1,0:T(8,128)S(1)}, u32[]{:S(2)}, u32[]{:S(2)}) %collective-permute-start.12) | collective-permute-done | bytes 262176 | tf_op jit(solution)/shard_map/ppermute | solution.py:568
  101.2 2.3 %shard_map.111 = (f32[2,4,256,256]{3,2,1,0:T(8,128)}, f32[2,4,256,256]{3,2,1,0:T(8,128)}) custom-call(s32[1]{0:T(128)} %bitcast.core_ref.core, f32[2,4,256,256]{3,2,1,0:T(8,128)S(1)} %copy-done.1, f32[2,4,256,256]{3,2,1,0:T(8,128)S(1)} %get-tuple-element.64.own, f32[2,4,64,256]{3,2,1,0:T(8,128)S(1)} %collective-permute-done.10.from_above, ...), custom_call_target="tpu_custom_call" | custom-call | bytes 1048576 | tf_op jit(solution)/shard_map/pallas_call | solution.py:515
  (26 shorter events, 0.5 us)
Async XLA Ops:
  0.6 38.1 %copy-start.8 = (f32[2,8,128]{2,1,0:T(8,128)S(1)}, f32[2,8,128]{2,1,0:T(8,128)}, u32[]{:S(2)}) copy-start(f32[2,8,128]{2,1,0:T(8,128)} %constant.27.clone.by_lane) | copy-start | bytes 24580
  0.7 1.6 %copy-start = (f32[2,4,256,256]{3,2,1,0:T(8,128)S(1)}, f32[2,4,256,256]{3,2,1,0:T(8,128)}, u32[]{:S(2)}) copy-start(f32[2,4,256,256]{3,2,1,0:T(8,128)} %obj.5) | copy-start | bytes 6291460
  2.2 36.5 %copy-start.1 = (f32[2,4,256,256]{3,2,1,0:T(8,128)S(1)}, f32[2,4,256,256]{3,2,1,0:T(8,128)}, u32[]{:S(2)}) copy-start(f32[2,4,256,256]{3,2,1,0:T(8,128)} %obj.5) | copy-start | bytes 6291460
  2.2 36.5 %copy-start.2 = (bf16[4,256,256]{2,1,0:T(8,128)(2,1)S(1)}, bf16[4,256,256]{2,1,0:T(8,128)(2,1)}, u32[]{:S(2)}) copy-start(bf16[4,256,256]{2,1,0:T(8,128)(2,1)} %constant.25.clone.mats) | copy-start | bytes 1572868
  2.6 12.3 %collective-permute-start.4 = (f32[4,256,128]{2,1,0:T(8,128)S(1)}, f32[4,256,128]{2,1,0:T(8,128)S(1)}, u32[]{:S(2)}, u32[]{:S(2)}) collective-permute-start(f32[4,256,128]{2,1,0:T(8,128)S(1)} %get-tuple-element.45), channel_id=1, source_target_pairs={{0,1},{1,0},{2,3},{3,2},{4,5},{5,4},{6,7},{7,6},{8,9},{9,8},{10,11... | collective-permute-start | bytes 1572872 | tf_op jit(solution)/shard_map/ppermute | solution.py:568
  3.4 31.8 %collective-permute-start = (f32[2,4,64,256]{3,2,1,0:T(8,128)S(1)}, f32[2,4,64,256]{3,2,1,0:T(8,128)S(1)}, u32[]{:S(2)}, u32[]{:S(2)}) collective-permute-start(f32[2,4,64,256]{3,2,1,0:T(8,128)S(1)} %get-tuple-element.41), channel_id=1, source_target_pairs={{0,240},{1,241},{2,242},{3,243},{4,244},{5,245},{6,246},{7,247},{8... | collective-permute-start | bytes 1572872 | tf_op jit(solution)/shard_map/ppermute | solution.py:568
  3.9 31.3 %collective-permute-start.1 = (f32[2,4,64,256]{3,2,1,0:T(8,128)S(1)}, f32[2,4,64,256]{3,2,1,0:T(8,128)S(1)}, u32[]{:S(2)}, u32[]{:S(2)}) collective-permute-start(f32[2,4,64,256]{3,2,1,0:T(8,128)S(1)} %get-tuple-element.42), channel_id=1, source_target_pairs={{0,16},{1,17},{2,18},{3,19},{4,20},{5,21},{6,22},{7,23},{8,24},{9,... | collective-permute-start | bytes 1572872 | tf_op jit(solution)/shard_map/ppermute | solution.py:568
  5.8 29.4 %collective-permute-start.2 = (f32[2,256,128]{2,1,0:T(8,128)S(1)}, f32[2,256,128]{2,1,0:T(8,128)S(1)}, u32[]{:S(2)}, u32[]{:S(2)}) collective-permute-start(f32[2,256,128]{2,1,0:T(8,128)S(1)} %get-tuple-element.43), channel_id=1, source_target_pairs={{0,15},{1,2},{2,1},{3,4},{4,3},{5,6},{6,5},{7,8},{8,7},{9,10},{10,... | collective-permute-start | bytes 786440 | tf_op jit(solution)/shard_map/ppermute | solution.py:568
  7.1 15.1 %collective-permute-start.3 = (f32[4,64,128]{2,1,0:T(8,128)S(1)}, f32[4,64,128]{2,1,0:T(8,128)S(1)}, u32[]{:S(2)}, u32[]{:S(2)}) collective-permute-start(f32[4,64,128]{2,1,0:T(8,128)S(1)} %get-tuple-element.44), channel_id=1, source_target_pairs={{0,255},{1,242},{2,241},{3,244},{4,243},{5,246},{6,245},{7,248},{8... | collective-permute-start | bytes 393224 | tf_op jit(solution)/shard_map/ppermute | solution.py:568
  14.9 20.3 %collective-permute-start.5 = (f32[4,64,128]{2,1,0:T(8,128)S(1)}, f32[4,64,128]{2,1,0:T(8,128)S(1)}, u32[]{:S(2)}, u32[]{:S(2)}) collective-permute-start(f32[4,64,128]{2,1,0:T(8,128)S(1)} %get-tuple-element.47), channel_id=1, source_target_pairs={{0,31},{1,18},{2,17},{3,20},{4,19},{5,22},{6,21},{7,24},{8,23},{9,... | collective-permute-start | bytes 393224 | tf_op jit(solution)/shard_map/ppermute | solution.py:568
  14.9 1.0 %copy-start.3 = (f32[2,256,256]{2,1,0:T(8,128)S(1)}, f32[2,256,256]{2,1,0:T(8,128)}, u32[]{:S(2)}) copy-start(f32[2,256,256]{2,1,0:T(8,128)} %probe_ref.1) | copy-start | bytes 1572868
  16.0 1.0 %copy-start.4 = (f32[1,1,2,256,256]{4,3,2,1,0:T(8,128)S(1)}, f32[1,1,2,256,256]{4,3,2,1,0:T(8,128)}, u32[]{:S(2)}) copy-start(f32[1,1,2,256,256]{4,3,2,1,0:T(8,128)} %param.11) | copy-start | bytes 1572868
  17.0 0.9 copy-start.5
  18.0 0.9 copy-start.6
  18.9 0.7 copy-start.9
  35.4 3.3 %collective-permute-start.6 = (f32[4,128,128]{2,1,0:T(8,128)S(1)}, f32[4,128,128]{2,1,0:T(8,128)S(1)}, u32[]{:S(2)}, u32[]{:S(2)}) collective-permute-start(f32[4,128,128]{2,1,0:T(8,128)S(1)} %get-tuple-element.50), channel_id=1, source_target_pairs={{0,1},{1,0},{2,3},{3,2},{4,5},{5,4},{6,7},{7,6},{8,9},{9,8},{10,11... | collective-permute-start | bytes 786440 | tf_op jit(solution)/shard_map/ppermute | solution.py:568
  35.5 9.9 %collective-permute-start.7 = (f32[2,256,128]{2,1,0:T(8,128)S(1)}, f32[2,256,128]{2,1,0:T(8,128)S(1)}, u32[]{:S(2)}, u32[]{:S(2)}) collective-permute-start(f32[2,256,128]{2,1,0:T(8,128)S(1)} %get-tuple-element.54), channel_id=1, source_target_pairs={{0,15},{1,2},{2,1},{3,4},{4,3},{5,6},{6,5},{7,8},{8,7},{9,10},{10,... | collective-permute-start | bytes 786440 | tf_op jit(solution)/shard_map/ppermute | solution.py:568
  38.8 0.9 copy-start.7
  52.9 9.5 %collective-permute-start.8 = (f32[2,256,128]{2,1,0:T(8,128)S(1)}, f32[2,256,128]{2,1,0:T(8,128)S(1)}, u32[]{:S(2)}, u32[]{:S(2)}) collective-permute-start(f32[2,256,128]{2,1,0:T(8,128)S(1)} %get-tuple-element.68), channel_id=1, source_target_pairs={{0,15},{1,2},{2,1},{3,4},{4,3},{5,6},{6,5},{7,8},{8,7},{9,10},{10,... | collective-permute-start | bytes 786440 | tf_op jit(solution)/shard_map/ppermute | solution.py:568
  62.3 2.5 %collective-permute-start.9 = (f32[4,384,128]{2,1,0:T(8,128)S(1)}, f32[4,384,128]{2,1,0:T(8,128)S(1)}, u32[]{:S(2)}, u32[]{:S(2)}) collective-permute-start(f32[4,384,128]{2,1,0:T(8,128)S(1)} %get-tuple-element.69), channel_id=1, source_target_pairs={{0,1},{1,0},{2,3},{3,2},{4,5},{5,4},{6,7},{7,6},{8,9},{9,8},{10,11... | collective-permute-start | bytes 2359304 | tf_op jit(solution)/shard_map/ppermute | solution.py:568
  65.1 36.1 %collective-permute-start.10 = (f32[2,4,64,256]{3,2,1,0:T(8,128)S(1)}, f32[2,4,64,256]{3,2,1,0:T(8,128)S(1)}, u32[]{:S(2)}, u32[]{:S(2)}) collective-permute-start(f32[2,4,64,256]{3,2,1,0:T(8,128)S(1)} %get-tuple-element.71), channel_id=1, source_target_pairs={{0,16},{1,17},{2,18},{3,19},{4,20},{5,21},{6,22},{7,23},{8,24},{9,... | collective-permute-start | bytes 1572872 | tf_op jit(solution)/shard_map/ppermute | solution.py:568
  68.0 33.2 %collective-permute-start.11 = (f32[2,4,64,256]{3,2,1,0:T(8,128)S(1)}, f32[2,4,64,256]{3,2,1,0:T(8,128)S(1)}, u32[]{:S(2)}, u32[]{:S(2)}) collective-permute-start(f32[2,4,64,256]{3,2,1,0:T(8,128)S(1)} %get-tuple-element.72), channel_id=1, source_target_pairs={{0,240},{1,241},{2,242},{3,243},{4,244},{5,245},{6,246},{7,247},{8... | collective-permute-start | bytes 1572872 | tf_op jit(solution)/shard_map/ppermute | solution.py:568
  68.0 33.2 %collective-permute-start.12 = (f32[2,256,128]{2,1,0:T(8,128)S(1)}, f32[2,256,128]{2,1,0:T(8,128)S(1)}, u32[]{:S(2)}, u32[]{:S(2)}) collective-permute-start(f32[2,256,128]{2,1,0:T(8,128)S(1)} %get-tuple-element.73), channel_id=1, source_target_pairs={{0,15},{1,2},{2,1},{3,4},{4,3},{5,6},{6,5},{7,8},{8,7},{9,10},{10,... | collective-permute-start | bytes 786440 | tf_op jit(solution)/shard_map/ppermute | solution.py:568
  72.7 9.4 %collective-permute-start.13 = (f32[4,64,128]{2,1,0:T(8,128)S(1)}, f32[4,64,128]{2,1,0:T(8,128)S(1)}, u32[]{:S(2)}, u32[]{:S(2)}) collective-permute-start(f32[4,64,128]{2,1,0:T(8,128)S(1)} %get-tuple-element.74), channel_id=1, source_target_pairs={{0,31},{1,18},{2,17},{3,20},{4,19},{5,22},{6,21},{7,24},{8,23},{9,... | collective-permute-start | bytes 393224 | tf_op jit(solution)/shard_map/ppermute | solution.py:568
  75.2 13.2 %collective-permute-start.14 = (f32[4,64,128]{2,1,0:T(8,128)S(1)}, f32[4,64,128]{2,1,0:T(8,128)S(1)}, u32[]{:S(2)}, u32[]{:S(2)}) collective-permute-start(f32[4,64,128]{2,1,0:T(8,128)S(1)} %get-tuple-element.75), channel_id=1, source_target_pairs={{0,255},{1,242},{2,241},{3,244},{4,243},{5,246},{6,245},{7,248},{8... | collective-permute-start | bytes 393224 | tf_op jit(solution)/shard_map/ppermute | solution.py:568
where the time goes:
time: 104 us
  waiting for transfers between devices  39.2 us (38%)
  starting transfers between devices  33 us (32%)
  Pallas kernels  23.4 us (22%)
  local copies, waits for them, and re-layouts  7.16 us (7%)
    ppermute x15, waiting for transfers between devices, send(): return lax.ppermute(x, AXES, route[way])  39.2 us
    ppermute x15, starting transfers between devices, send(): return lax.ppermute(x, AXES, route[way])  33 us
    pallas_call x8, Pallas kernels, call(): pl.pallas_call(kernel, out_shape=shapes, in_specs=[SMEM] * scalars + (pla...  23.4 us
    unnamed x20, local copies, waits for them, and re-layouts  7.16 us
  transfers between devices with their start and end apart: 15, of which 7 were waited for; matrix products, arithmetic and copies ran while one was open for 0% of the time, Pallas kernels for 13%

commit v1 on v0

--- a/solution.py
+++ b/solution.py
@@ -79,18 +79,22 @@
     return jnp.where(low, swap(im1), re1)
 
 
-def pack_kernel(core_ref, object_ref, top, bottom, out_first, out_last, out_top, out_bottom, in_rows):
+def pack_kernel(core_ref, object_ref, top, bottom, out_first, out_last, out_top, out_bottom, band, arrived):
     core = core_ref[0]
+    lane = pl.multiple_of(core * HALF, HALF)
+    rows = [
+        pltpu.make_async_copy(object_ref.at[:, :, :HALO], top, arrived.at[0]),
+        pltpu.make_async_copy(object_ref.at[:, :, W - HALO :], bottom, arrived.at[1]),
+    ]
+    columns = pltpu.make_async_copy(object_ref.at[:, :, :, pl.ds(lane, HALF)], band, arrived.at[2])
+    columns.start()
+    for copy in rows:
+        copy.start()
+    columns.wait()
     for s in range(4):
-        for c in range(2):
-            top[c, s] = object_ref[c, s, :HALO, :]
-            bottom[c, s] = object_ref[c, s, W - HALO :, :]
         for r in range(0, W, 64):
-            re, im = object_ref[0, s, r : r + 64, :], object_ref[1, s, r : r + 64, :]
-            left = pack_left(re[:, :HALF], im[:, :HALF])
-            right = pack_right(re[:, HALF:], im[:, HALF:])
-            packed = jnp.where(core == 1, right, left)
-            in_rows[s, r : r + 64, :] = jnp.where(core == 1, left, right)
+            re, im = band[0, s, r : r + 64], band[1, s, r : r + 64]
+            packed = jnp.where(core == 1, pack_right(re, im), pack_left(re, im))
             if s < PARTED:
                 out_first[s, r : r + 64, :] = packed
             else:
@@ -99,17 +103,24 @@
                 out_top[s] = packed
             if r == W - HALO:
                 out_bottom[s] = packed
-
-
-def relay_kernel(core_ref, below_ref, above_ref, last_ref, first_ref, corner_below, corner_above, measured, inward, last):
+    for copy in rows:
+        copy.wait()
+
+
+def relay_kernel(core_ref, object_ref, below_ref, above_ref, last_ref, first_ref, corner_below, corner_above, measured,
+                 inward, last):
     core = core_ref[0]
     last[...] = last_ref[...]
     for s in range(4):
-        for at, ref in ((0, below_ref), (HALO, above_ref)):
-            re, im = ref[0, s], ref[1, s]
+        for r in range(0, 384, 64):
+            if r < W:
+                re, im = object_ref[0, s, r : r + 64], object_ref[1, s, r : r + 64]
+            else:
+                ref = below_ref if r == W else above_ref
+                re, im = ref[0, s], ref[1, s]
             left = pack_left(re[:, :HALF], im[:, :HALF])
             right = pack_right(re[:, HALF:], im[:, HALF:])
-            inward[s, at : at + HALO, :] = jnp.where(core == 1, left, right)
+            inward[s, r : r + 64, :] = jnp.where(core == 1, left, right)
 
 
 def prepare(pos_ref, probe_ref, propagator_ref, intensity_ref, order_ref, wave_ref, phase_ref, measured_ref):
@@ -261,7 +272,7 @@
     def __init__(self, pos_ref, core_ref, refs, side, at):
         self.at = at
         self.core = core_ref[0]
-        self.object, self.below, self.above, self.out, self.out_below, self.out_above, self.inner, self.in_rows = refs
+        self.object, self.below, self.above, self.out, self.out_below, self.out_above, self.inner = refs
         self.side = side
         self.shift = [(pos_ref[k, 0] - HALO, pos_ref[k, 1] - HALO) for k in range(2)]
 
@@ -271,7 +282,7 @@
                 outer = self.out[s - self.at, r : r + 64]
             else:
                 outer = (self.out_below if r == W else self.out_above)[s]
-            inner = self.in_rows[s, r : r + 64] if r < W else self.inner[s, r - W : r - W + 64]
+            inner = self.inner[s, r : r + 64]
             right = jnp.where(self.core == 1, outer, inner)
             left = jnp.where(self.core == 1, inner, outer)
             low = lanes(64) < HALO
@@ -414,19 +425,19 @@
     lax.fori_loop(0, high - low, slice_step, 0)
 
 
-def forward_kernel(pos, core, waves_in, phase, obj, below, above, out, out_below, out_above, inner, in_rows,
-                   mats, by_row, by_lane, waves, seen, xr_h, xr_l, xl_h, xl_l, wr, wl, side):
+def forward_kernel(pos, core, waves_in, phase, obj, below, above, out, out_below, out_above, inner, mats, by_row, by_lane,
+                   waves, seen, xr_h, xr_l, xl_h, xl_l, wr, wl, side):
     t = Transform((mats, by_row, by_lane), (xr_h, xr_l, xl_h, xl_l, wr, wl))
-    w = Windows(pos, core, (obj, below, above, out, out_below, out_above, inner, in_rows), side, 0)
+    w = Windows(pos, core, (obj, below, above, out, out_below, out_above, inner), side, 0)
     forward_slices(t, w, waves, seen, phase, 0, PARTED)
 
 
 def turn_kernel(pos, core, waves_in, seen_in, phase, measured, obj, below, above, out, out_below, out_above, inner,
-                in_rows, mats, by_row, by_lane,
+                mats, by_row, by_lane,
                 waves, seen, back, own, g_below, g_above, g_out_below, g_out_above, g_inner, g_out,
                 xr_h, xr_l, xl_h, xl_l, wr, wl, side):
     t = Transform((mats, by_row, by_lane), (xr_h, xr_l, xl_h, xl_l, wr, wl))
-    w = Windows(pos, core, (obj, below, above, out, out_below, out_above, inner, in_rows), side, PARTED)
+    w = Windows(pos, core, (obj, below, above, out, out_below, out_above, inner), side, PARTED)
     f = Folding(pos, core, (own, g_below, g_above, g_out, g_out_below, g_out_above, g_inner), PARTED)
     forward_slices(t, w, waves, seen, phase, PARTED, 3)
     w.gather_sides(3)
@@ -561,14 +572,19 @@
     core = (lax.axis_index("col") % 2).astype(jnp.int32).reshape(1)
     pos = positions[0, 0]
     flops = 2 * 2 * 8 * 3 * 2 * W**3 // 2
-    bands, corners, columns, both = (2, 4, HALO, W), (4, HALO, HALF), (4, W, HALF), (4, 2 * HALO, HALF)
+    bands, corners, columns = (2, 4, HALO, W), (4, HALO, HALF), (4, 384, HALF)
     first, last = (PARTED, W, HALF), (4 - PARTED, W, HALF)
 
     def send(x, way):
         return lax.ppermute(x, AXES, route[way])
 
-    top, bottom, out_first, out_last, out_top, out_bottom, in_rows = call(
-        pack_kernel, [bands, bands, first, last, corners, corners, columns], (core, obj), 1
+    top, bottom, out_first, out_last, out_top, out_bottom = call(
+        pack_kernel,
+        [bands, bands, first, last, corners, corners],
+        (core, obj),
+        1,
+        [pltpu.VMEM((2, 4, W, HALF), F32), pltpu.SemaphoreType.DMA((3,))],
+        places=[HBM],
     )
     waves, phase, measured = call(
         prepare,
@@ -576,16 +592,15 @@
         (pos, probe, propagator, intensities[0, 0], order),
         1,
     )
-    in_rows, out_bottom = lax.optimization_barrier((send(in_rows, "in"), out_bottom))
     below, above = send(top, "up"), send(bottom, "down")
     out_first = send(out_first, "out")
     corner_below, corner_above = send(out_top, "out_up"), send(out_bottom, "out_down")
     inward, out_last = call(
         relay_kernel,
-        [both, last],
-        (core, below, above, out_last, out_first, corner_below, corner_above, measured),
+        [columns, last],
+        (core, obj, below, above, out_last, out_first, corner_below, corner_above, measured),
         1,
-        places=[VMEM] * 3 + [ANYWHERE] * 4,
+        places=[VMEM] * 4 + [ANYWHERE] * 4,
     )
     out_last = send(out_last, "out")
     inner = send(inward, "in")
@@ -593,17 +608,17 @@
     waves, seen = call(
         forward_kernel,
         [STACK, STACK],
-        (pos, core, waves, phase, obj, below, above, out_first, corner_below, corner_above, inner, in_rows, *tables),
+        (pos, core, waves, phase, obj, below, above, out_first, corner_below, corner_above, inner, *tables),
         2,
         TRANSFORM_SCRATCH + [SIDE_SCRATCH],
         flops=PARTED * flops,
         aliases={2: 0},
     )
-    sums = [(2, 4, W, W), bands, bands, corners, corners, (4, 384, HALF)]
+    sums = [(2, 4, W, W), bands, bands, corners, corners, columns]
     waves, seen, back, *terms, out_last = call(
         turn_kernel,
         [STACK, STACK, (2, 2, W, W), *sums, last],
-        (pos, core, waves, seen, phase, measured, obj, below, above, out_last, corner_below, corner_above, inner, in_rows, *tables),
+        (pos, core, waves, seen, phase, measured, obj, below, above, out_last, corner_below, corner_above, inner, *tables),
         2,
         TRANSFORM_SCRATCH + [SIDE_SCRATCH],
         flops=(7 - 2 * PARTED) * flops,

time: 104 us -> 103 us (level)
  starting transfers between devices: 33 us -> 34.1 us
    ppermute x15 -> x14, starting transfers between devices: 33 us -> 34.1 us  [send(): return lax.ppermute(x, AXES, route[way])]
    ppermute x15 -> x14, waiting for transfers between devices: 39.2 us -> 38.3 us  [send(): return lax.ppermute(x, AXES, route[way])]
  transfers between devices with their start and end apart: 15 -> 14, of which waited for: 7 -> 7; matrix products, arithmetic and copies ran while one was open for 0% -> 0% of each run, Pallas kernels for 13% -> 12%
where the time goes in v1:
time: 103 us
  waiting for transfers between devices  38.3 us (37%)
  starting transfers between devices  34.1 us (33%)
  Pallas kernels  23.5 us (23%)
  local copies, waits for them, and re-layouts  6.26 us (6%)
    ppermute x14, waiting for transfers between devices, send(): return lax.ppermute(x, AXES, route[way])  38.3 us
    ppermute x14, starting transfers between devices, send(): return lax.ppermute(x, AXES, route[way])  34.1 us
    pallas_call x8, Pallas kernels, call(): pl.pallas_call(kernel, out_shape=shapes, in_specs=[SMEM] * scalars + (pla...  23.5 us
    unnamed x20, local copies, waits for them, and re-layouts  6.26 us
  transfers between devices with their start and end apart: 14, of which 7 were waited for; matrix products, arithmetic and copies ran while one was open for 0% of the time, Pallas kernels for 12%

profile of v1, /device:TPU:31, one launch (start us, length us, event | category | flops | bytes accessed | tf_op | source)
XLA Modules:
  0.0 103.0 jit_solution(5275406179559988110)
XLA Ops:
  0.7 1.6 %copy-done = f32[2,4,256,256]{3,2,1,0:T(8,128)S(1)} copy-done((f32[2,4,256,256]{3,2,1,0:T(8,128)S(1)}, f32[2,4,256,256]{3,2,1,0:T(8,128)}, u32[]{:S(2)}) %copy-start) | copy-done | bytes 2097176
  2.2 0.4 shard_map.105
  2.6 0.6 collective-permute-start
  3.3 1.8 %collective-permute-start.1 = (f32[2,4,64,256]{3,2,1,0:T(8,128)S(1)}, f32[2,4,64,256]{3,2,1,0:T(8,128)S(1)}, u32[]{:S(2)}, u32[]{:S(2)}) collective-permute-start(f32[2,4,64,256]{3,2,1,0:T(8,128)S(1)} %get-tuple-element.39), channel_id=1, source_target_pairs={{0,16},{1,17},{2,18},{3,19},{4,20},{5,21},{6,22},{7,23},{8,24},{9,... | collective-permute-start | bytes 1572872 | tf_op jit(solution)/shard_map/ppermute | solution.py:579
  5.1 1.9 %collective-permute-start.2 = (f32[2,256,128]{2,1,0:T(8,128)S(1)}, f32[2,256,128]{2,1,0:T(8,128)S(1)}, u32[]{:S(2)}, u32[]{:S(2)}) collective-permute-start(f32[2,256,128]{2,1,0:T(8,128)S(1)} %get-tuple-element.40), channel_id=1, source_target_pairs={{0,15},{1,2},{2,1},{3,4},{4,3},{5,6},{6,5},{7,8},{8,7},{9,10},{10,... | collective-permute-start | bytes 786440 | tf_op jit(solution)/shard_map/ppermute | solution.py:579
  7.0 7.3 %collective-permute-start.3 = (f32[4,64,128]{2,1,0:T(8,128)S(1)}, f32[4,64,128]{2,1,0:T(8,128)S(1)}, u32[]{:S(2)}, u32[]{:S(2)}) collective-permute-start(f32[4,64,128]{2,1,0:T(8,128)S(1)} %get-tuple-element.41), channel_id=1, source_target_pairs={{0,255},{1,242},{2,241},{3,244},{4,243},{5,246},{6,245},{7,248},{8... | collective-permute-start | bytes 393224 | tf_op jit(solution)/shard_map/ppermute | solution.py:579
  14.3 1.0 %copy-done.3 = f32[2,256,256]{2,1,0:T(8,128)S(1)} copy-done((f32[2,256,256]{2,1,0:T(8,128)S(1)}, f32[2,256,256]{2,1,0:T(8,128)}, u32[]{:S(2)}) %copy-start.3) | copy-done | bytes 524312
  15.3 1.0 %copy-done.4 = f32[1,1,2,256,256]{4,3,2,1,0:T(8,128)S(1)} copy-done((f32[1,1,2,256,256]{4,3,2,1,0:T(8,128)S(1)}, f32[1,1,2,256,256]{4,3,2,1,0:T(8,128)}, u32[]{:S(2)}) %copy-start.4) | copy-done | bytes 524312
  16.3 0.9 copy-done.5
  17.3 0.9 copy-done.6
  18.2 0.7 copy-done.9
  18.9 2.6 %shard_map.104 = (f32[4,2,2,256,256]{4,3,2,1,0:T(8,128)S(1)}, f32[2,256,256]{2,1,0:T(8,128)S(1)}, f32[2,256,256]{2,1,0:T(8,128)S(1)}) custom-call(s32[2,2]{1,0:T(2,128)S(1)} %bitcast.4, f32[2,256,256]{2,1,0:T(8,128)S(1)} %copy-done.3, f32[256,256]{1,0:T(8,128)S(1)} %copy-done.5, f32[2,256,256]{2,1,0:T(8,128)S(1)} %bitcast.3, bf16[2,256,256]{2,1,0:T(8,128)(2,1)S(1)} %copy-done.6), custom_call_target="tpu_custom_call" | custom-call | bytes 1048576 | tf_op jit(solution)/shard_map/pallas_call | solution.py:526
  21.5 0.5 collective-permute-done.4.corner_above.out_above
  22.0 10.6 %collective-permute-done.2.first_ref.out = f32[2,256,128]{2,1,0:T(8,128)S(1)} collective-permute-done((f32[2,256,128]{2,1,0:T(8,128)S(1)}, f32[2,256,128]{2,1,0:T(8,128)S(1)}, u32[]{:S(2)}, u32[]{:S(2)}) %collective-permute-start.2) | collective-permute-done | bytes 262176 | tf_op jit(solution)/shard_map/ppermute | solution.py:579
  32.5 0.5 shard_map.106
  33.0 0.2 collective-permute-start.5
  33.2 4.4 %collective-permute-start.6 = (f32[2,256,128]{2,1,0:T(8,128)S(1)}, f32[2,256,128]{2,1,0:T(8,128)S(1)}, u32[]{:S(2)}, u32[]{:S(2)}) collective-permute-start(f32[2,256,128]{2,1,0:T(8,128)S(1)} %get-tuple-element.48), channel_id=1, source_target_pairs={{0,15},{1,2},{2,1},{3,4},{4,3},{5,6},{6,5},{7,8},{8,7},{9,10},{10,... | collective-permute-start | bytes 786440 | tf_op jit(solution)/shard_map/ppermute | solution.py:579
  37.7 5.1 %shard_map.107 = (f32[4,2,2,256,256]{4,3,2,1,0:T(8,128)S(1)}, f32[4,2,2,256,256]{4,3,2,1,0:T(8,128)S(1)}) custom-call(s32[2,2]{1,0:T(2,128)S(1)} %bitcast.5, s32[1]{0:T(128)} %bitcast.core_ref.core, f32[4,2,2,256,256]{4,3,2,1,0:T(8,128)S(1)} %get-tuple-element.36.waves_in, ...), custom_call_target="tpu_custom_call", output_to_operand_aliasing={{0}: (2, {})} | custom-call | flops 3221225472 | bytes 1048576 | tf_op jit(solution)/shard_map/pallas_call | solution.py:526
  42.7 1.6 %collective-permute-done.6.out = f32[2,256,128]{2,1,0:T(8,128)S(1)} collective-permute-done((f32[2,256,128]{2,1,0:T(8,128)S(1)}, f32[2,256,128]{2,1,0:T(8,128)S(1)}, u32[]{:S(2)}, u32[]{:S(2)}) %collective-permute-start.6) | collective-permute-done | bytes 262176 | tf_op jit(solution)/shard_map/ppermute | solution.py:579
  44.3 7.3 %shard_map.108 = (f32[4,2,2,256,256]{4,3,2,1,0:T(8,128)S(1)}, f32[4,2,2,256,256]{4,3,2,1,0:T(8,128)S(1)}, f32[2,2,256,256]{3,2,1,0:T(8,128)S(1)}, f32[2,4,256,25...) custom-call(s32[2,2]{1,0:T(2,128)S(1)} %bitcast.6, ...), custom_call_target="tpu_custom_call", output_to_operand_aliasing={{0}: (2, {}), {1}: (3, {})} | custom-call | flops 4831838208 | bytes 1048576 | tf_op jit(solution)/shard_map/pallas_call | solution.py:526
  51.6 4.7 %collective-permute-start.7 = (f32[2,256,128]{2,1,0:T(8,128)S(1)}, f32[2,256,128]{2,1,0:T(8,128)S(1)}, u32[]{:S(2)}, u32[]{:S(2)}) collective-permute-start(f32[2,256,128]{2,1,0:T(8,128)S(1)} %get-tuple-element.62), channel_id=1, source_target_pairs={{0,15},{1,2},{2,1},{3,4},{4,3},{5,6},{6,5},{7,8},{8,7},{9,10},{10,... | collective-permute-start | bytes 786440 | tf_op jit(solution)/shard_map/ppermute | solution.py:579
  56.3 5.2 %shard_map.109 = (f32[2,2,256,256]{3,2,1,0:T(8,128)S(1)}, f32[2,4,256,256]{3,2,1,0:T(8,128)S(1)}, f32[2,4,64,256]{3,2,1,0:T(8,128)S(1)}, f32[2,4,64,256]{3,2,1,0...) custom-call(s32[2,2]{1,0:T(2,128)S(1)} %bitcast.7, ...), custom_call_target="tpu_custom_call", output_to_operand_aliasing={{0}: (2, {}), {1}: (6, {}), {2}: (7, {}), {3}: (8, {}), {4}... | custom-call | flops 3221225472 | bytes 1048576 | tf_op jit(solution)/shard_map/pallas_call | solution.py:526
  61.6 0.3 collective-permute-start.8
  61.9 2.3 %collective-permute-done.8.inner = f32[4,384,128]{2,1,0:T(8,128)S(1)} collective-permute-done((f32[4,384,128]{2,1,0:T(8,128)S(1)}, f32[4,384,128]{2,1,0:T(8,128)S(1)}, u32[]{:S(2)}, u32[]{:S(2)}) %collective-permute-start.8) | collective-permute-done | bytes 786464 | tf_op jit(solution)/shard_map/ppermute | solution.py:579
  64.4 3.0 %collective-permute-start.9 = (f32[2,4,64,256]{3,2,1,0:T(8,128)S(1)}, f32[2,4,64,256]{3,2,1,0:T(8,128)S(1)}, u32[]{:S(2)}, u32[]{:S(2)}) collective-permute-start(f32[2,4,64,256]{3,2,1,0:T(8,128)S(1)} %get-tuple-element.65), channel_id=1, source_target_pairs={{0,16},{1,17},{2,18},{3,19},{4,20},{5,21},{6,22},{7,23},{8,24},{9,... | collective-permute-start | bytes 1572872 | tf_op jit(solution)/shard_map/ppermute | solution.py:579
  67.4 4.8 %collective-permute-start.11 = (f32[2,256,128]{2,1,0:T(8,128)S(1)}, f32[2,256,128]{2,1,0:T(8,128)S(1)}, u32[]{:S(2)}, u32[]{:S(2)}) collective-permute-start(f32[2,256,128]{2,1,0:T(8,128)S(1)} %get-tuple-element.67), channel_id=1, source_target_pairs={{0,15},{1,2},{2,1},{3,4},{4,3},{5,6},{6,5},{7,8},{8,7},{9,10},{10,... | collective-permute-start | bytes 786440 | tf_op jit(solution)/shard_map/ppermute | solution.py:579
  72.1 2.4 %collective-permute-start.12 = (f32[4,64,128]{2,1,0:T(8,128)S(1)}, f32[4,64,128]{2,1,0:T(8,128)S(1)}, u32[]{:S(2)}, u32[]{:S(2)}) collective-permute-start(f32[4,64,128]{2,1,0:T(8,128)S(1)} %get-tuple-element.68), channel_id=1, source_target_pairs={{0,31},{1,18},{2,17},{3,20},{4,19},{5,22},{6,21},{7,24},{8,23},{9,... | collective-permute-start | bytes 393224 | tf_op jit(solution)/shard_map/ppermute | solution.py:579
  74.5 2.7 %collective-permute-start.13 = (f32[4,64,128]{2,1,0:T(8,128)S(1)}, f32[4,64,128]{2,1,0:T(8,128)S(1)}, u32[]{:S(2)}, u32[]{:S(2)}) collective-permute-start(f32[4,64,128]{2,1,0:T(8,128)S(1)} %get-tuple-element.69), channel_id=1, source_target_pairs={{0,255},{1,242},{2,241},{3,244},{4,243},{5,246},{6,245},{7,248},{8... | collective-permute-start | bytes 393224 | tf_op jit(solution)/shard_map/ppermute | solution.py:579
  77.2 4.3 %collective-permute-done.12.out_above = f32[4,64,128]{2,1,0:T(8,128)S(1)} collective-permute-done((f32[4,64,128]{2,1,0:T(8,128)S(1)}, f32[4,64,128]{2,1,0:T(8,128)S(1)}, u32[]{:S(2)}, u32[]{:S(2)}) %collective-permute-start.12) | collective-permute-done | bytes 131104 | tf_op jit(solution)/shard_map/ppermute | solution.py:579
  81.4 6.4 %collective-permute-done.13.out_below = f32[4,64,128]{2,1,0:T(8,128)S(1)} collective-permute-done((f32[4,64,128]{2,1,0:T(8,128)S(1)}, f32[4,64,128]{2,1,0:T(8,128)S(1)}, u32[]{:S(2)}, u32[]{:S(2)}) %collective-permute-start.13) | collective-permute-done | bytes 131104 | tf_op jit(solution)/shard_map/ppermute | solution.py:579
  87.8 12.8 %collective-permute-done.11.out_first = f32[2,256,128]{2,1,0:T(8,128)S(1)} collective-permute-done((f32[2,256,128]{2,1,0:T(8,128)S(1)}, f32[2,256,128]{2,1,0:T(8,128)S(1)}, u32[]{:S(2)}, u32[]{:S(2)}) %collective-permute-start.11) | collective-permute-done | bytes 262176 | tf_op jit(solution)/shard_map/ppermute | solution.py:579
  100.6 2.2 %shard_map.111 = (f32[2,4,256,256]{3,2,1,0:T(8,128)}, f32[2,4,256,256]{3,2,1,0:T(8,128)}) custom-call(s32[1]{0:T(128)} %bitcast.core_ref.core, f32[2,4,256,256]{3,2,1,0:T(8,128)S(1)} %copy-done.1, f32[2,4,256,256]{3,2,1,0:T(8,128)S(1)} %get-tuple-element.58.own, f32[2,4,64,256]{3,2,1,0:T(8,128)S(1)} %collective-permute-done.9.from_above, ...), custom_call_target="tpu_custom_call" | custom-call | bytes 1048576 | tf_op jit(solution)/shard_map/pallas_call | solution.py:526
  (24 shorter events, 0.3 us)
Async XLA Ops:
  0.6 37.0 %copy-start.8 = (f32[2,8,128]{2,1,0:T(8,128)S(1)}, f32[2,8,128]{2,1,0:T(8,128)}, u32[]{:S(2)}) copy-start(f32[2,8,128]{2,1,0:T(8,128)} %constant.27.clone.by_lane) | copy-start | bytes 24580
  0.7 1.6 %copy-start = (f32[2,4,256,256]{3,2,1,0:T(8,128)S(1)}, f32[2,4,256,256]{3,2,1,0:T(8,128)}, u32[]{:S(2)}) copy-start(f32[2,4,256,256]{3,2,1,0:T(8,128)} %obj.5) | copy-start | bytes 6291460
  2.2 30.3 %copy-start.1 = (f32[2,4,256,256]{3,2,1,0:T(8,128)S(1)}, f32[2,4,256,256]{3,2,1,0:T(8,128)}, u32[]{:S(2)}) copy-start(f32[2,4,256,256]{3,2,1,0:T(8,128)} %obj.5) | copy-start | bytes 6291460
  2.2 35.4 %copy-start.2 = (bf16[4,256,256]{2,1,0:T(8,128)(2,1)S(1)}, bf16[4,256,256]{2,1,0:T(8,128)(2,1)}, u32[]{:S(2)}) copy-start(bf16[4,256,256]{2,1,0:T(8,128)(2,1)} %constant.25.clone.mats) | copy-start | bytes 1572868
  2.6 29.9 %collective-permute-start = (f32[2,4,64,256]{3,2,1,0:T(8,128)S(1)}, f32[2,4,64,256]{3,2,1,0:T(8,128)S(1)}, u32[]{:S(2)}, u32[]{:S(2)}) collective-permute-start(f32[2,4,64,256]{3,2,1,0:T(8,128)S(1)} %get-tuple-element.38), channel_id=1, source_target_pairs={{0,240},{1,241},{2,242},{3,243},{4,244},{5,245},{6,246},{7,247},{8... | collective-permute-start | bytes 1572872 | tf_op jit(solution)/shard_map/ppermute | solution.py:579
  3.3 29.3 %collective-permute-start.1 = (f32[2,4,64,256]{3,2,1,0:T(8,128)S(1)}, f32[2,4,64,256]{3,2,1,0:T(8,128)S(1)}, u32[]{:S(2)}, u32[]{:S(2)}) collective-permute-start(f32[2,4,64,256]{3,2,1,0:T(8,128)S(1)} %get-tuple-element.39), channel_id=1, source_target_pairs={{0,16},{1,17},{2,18},{3,19},{4,20},{5,21},{6,22},{7,23},{8,24},{9,... | collective-permute-start | bytes 1572872 | tf_op jit(solution)/shard_map/ppermute | solution.py:579
  5.1 27.5 %collective-permute-start.2 = (f32[2,256,128]{2,1,0:T(8,128)S(1)}, f32[2,256,128]{2,1,0:T(8,128)S(1)}, u32[]{:S(2)}, u32[]{:S(2)}) collective-permute-start(f32[2,256,128]{2,1,0:T(8,128)S(1)} %get-tuple-element.40), channel_id=1, source_target_pairs={{0,15},{1,2},{2,1},{3,4},{4,3},{5,6},{6,5},{7,8},{8,7},{9,10},{10,... | collective-permute-start | bytes 786440 | tf_op jit(solution)/shard_map/ppermute | solution.py:579
  7.0 14.5 %collective-permute-start.3 = (f32[4,64,128]{2,1,0:T(8,128)S(1)}, f32[4,64,128]{2,1,0:T(8,128)S(1)}, u32[]{:S(2)}, u32[]{:S(2)}) collective-permute-start(f32[4,64,128]{2,1,0:T(8,128)S(1)} %get-tuple-element.41), channel_id=1, source_target_pairs={{0,255},{1,242},{2,241},{3,244},{4,243},{5,246},{6,245},{7,248},{8... | collective-permute-start | bytes 393224 | tf_op jit(solution)/shard_map/ppermute | solution.py:579
  14.3 7.7 %collective-permute-start.4 = (f32[4,64,128]{2,1,0:T(8,128)S(1)}, f32[4,64,128]{2,1,0:T(8,128)S(1)}, u32[]{:S(2)}, u32[]{:S(2)}) collective-permute-start(f32[4,64,128]{2,1,0:T(8,128)S(1)} %get-tuple-element.42), channel_id=1, source_target_pairs={{0,31},{1,18},{2,17},{3,20},{4,19},{5,22},{6,21},{7,24},{8,23},{9,... | collective-permute-start | bytes 393224 | tf_op jit(solution)/shard_map/ppermute | solution.py:579
  14.3 1.0 %copy-start.3 = (f32[2,256,256]{2,1,0:T(8,128)S(1)}, f32[2,256,256]{2,1,0:T(8,128)}, u32[]{:S(2)}) copy-start(f32[2,256,256]{2,1,0:T(8,128)} %probe_ref.1) | copy-start | bytes 1572868
  15.3 1.0 %copy-start.4 = (f32[1,1,2,256,256]{4,3,2,1,0:T(8,128)S(1)}, f32[1,1,2,256,256]{4,3,2,1,0:T(8,128)}, u32[]{:S(2)}) copy-start(f32[1,1,2,256,256]{4,3,2,1,0:T(8,128)} %param.11) | copy-start | bytes 1572868
  16.3 0.9 copy-start.5
  17.3 0.9 copy-start.6
  18.2 0.7 copy-start.9
  18.9 18.8 %copy-start.7 = (f32[2,128,128]{2,1,0:T(8,128)S(1)}, f32[2,128,128]{2,1,0:T(8,128)}, u32[]{:S(2)}) copy-start(f32[2,128,128]{2,1,0:T(8,128)} %constant.26.clone.by_row) | copy-start | bytes 393220
  33.0 4.6 %collective-permute-start.5 = (f32[4,384,128]{2,1,0:T(8,128)S(1)}, f32[4,384,128]{2,1,0:T(8,128)S(1)}, u32[]{:S(2)}, u32[]{:S(2)}) collective-permute-start(f32[4,384,128]{2,1,0:T(8,128)S(1)} %get-tuple-element.45), channel_id=1, source_target_pairs={{0,1},{1,0},{2,3},{3,2},{4,5},{5,4},{6,7},{7,6},{8,9},{9,8},{10,11... | collective-permute-start | bytes 2359304 | tf_op jit(solution)/shard_map/ppermute | solution.py:579
  33.2 11.1 %collective-permute-start.6 = (f32[2,256,128]{2,1,0:T(8,128)S(1)}, f32[2,256,128]{2,1,0:T(8,128)S(1)}, u32[]{:S(2)}, u32[]{:S(2)}) collective-permute-start(f32[2,256,128]{2,1,0:T(8,128)S(1)} %get-tuple-element.48), channel_id=1, source_target_pairs={{0,15},{1,2},{2,1},{3,4},{4,3},{5,6},{6,5},{7,8},{8,7},{9,10},{10,... | collective-permute-start | bytes 786440 | tf_op jit(solution)/shard_map/ppermute | solution.py:579
  51.6 9.9 %collective-permute-start.7 = (f32[2,256,128]{2,1,0:T(8,128)S(1)}, f32[2,256,128]{2,1,0:T(8,128)S(1)}, u32[]{:S(2)}, u32[]{:S(2)}) collective-permute-start(f32[2,256,128]{2,1,0:T(8,128)S(1)} %get-tuple-element.62), channel_id=1, source_target_pairs={{0,15},{1,2},{2,1},{3,4},{4,3},{5,6},{6,5},{7,8},{8,7},{9,10},{10,... | collective-permute-start | bytes 786440 | tf_op jit(solution)/shard_map/ppermute | solution.py:579
  61.6 2.6 %collective-permute-start.8 = (f32[4,384,128]{2,1,0:T(8,128)S(1)}, f32[4,384,128]{2,1,0:T(8,128)S(1)}, u32[]{:S(2)}, u32[]{:S(2)}) collective-permute-start(f32[4,384,128]{2,1,0:T(8,128)S(1)} %get-tuple-element.63), channel_id=1, source_target_pairs={{0,1},{1,0},{2,3},{3,2},{4,5},{5,4},{6,7},{7,6},{8,9},{9,8},{10,11... | collective-permute-start | bytes 2359304 | tf_op jit(solution)/shard_map/ppermute | solution.py:579
  64.4 36.2 %collective-permute-start.9 = (f32[2,4,64,256]{3,2,1,0:T(8,128)S(1)}, f32[2,4,64,256]{3,2,1,0:T(8,128)S(1)}, u32[]{:S(2)}, u32[]{:S(2)}) collective-permute-start(f32[2,4,64,256]{3,2,1,0:T(8,128)S(1)} %get-tuple-element.65), channel_id=1, source_target_pairs={{0,16},{1,17},{2,18},{3,19},{4,20},{5,21},{6,22},{7,23},{8,24},{9,... | collective-permute-start | bytes 1572872 | tf_op jit(solution)/shard_map/ppermute | solution.py:579
  67.4 33.3 %collective-permute-start.10 = (f32[2,4,64,256]{3,2,1,0:T(8,128)S(1)}, f32[2,4,64,256]{3,2,1,0:T(8,128)S(1)}, u32[]{:S(2)}, u32[]{:S(2)}) collective-permute-start(f32[2,4,64,256]{3,2,1,0:T(8,128)S(1)} %get-tuple-element.66), channel_id=1, source_target_pairs={{0,240},{1,241},{2,242},{3,243},{4,244},{5,245},{6,246},{7,247},{8... | collective-permute-start | bytes 1572872 | tf_op jit(solution)/shard_map/ppermute | solution.py:579
  67.4 33.3 %collective-permute-start.11 = (f32[2,256,128]{2,1,0:T(8,128)S(1)}, f32[2,256,128]{2,1,0:T(8,128)S(1)}, u32[]{:S(2)}, u32[]{:S(2)}) collective-permute-start(f32[2,256,128]{2,1,0:T(8,128)S(1)} %get-tuple-element.67), channel_id=1, source_target_pairs={{0,15},{1,2},{2,1},{3,4},{4,3},{5,6},{6,5},{7,8},{8,7},{9,10},{10,... | collective-permute-start | bytes 786440 | tf_op jit(solution)/shard_map/ppermute | solution.py:579
  72.1 9.3 %collective-permute-start.12 = (f32[4,64,128]{2,1,0:T(8,128)S(1)}, f32[4,64,128]{2,1,0:T(8,128)S(1)}, u32[]{:S(2)}, u32[]{:S(2)}) collective-permute-start(f32[4,64,128]{2,1,0:T(8,128)S(1)} %get-tuple-element.68), channel_id=1, source_target_pairs={{0,31},{1,18},{2,17},{3,20},{4,19},{5,22},{6,21},{7,24},{8,23},{9,... | collective-permute-start | bytes 393224 | tf_op jit(solution)/shard_map/ppermute | solution.py:579
  74.5 13.3 %collective-permute-start.13 = (f32[4,64,128]{2,1,0:T(8,128)S(1)}, f32[4,64,128]{2,1,0:T(8,128)S(1)}, u32[]{:S(2)}, u32[]{:S(2)}) collective-permute-start(f32[4,64,128]{2,1,0:T(8,128)S(1)} %get-tuple-element.69), channel_id=1, source_target_pairs={{0,255},{1,242},{2,241},{3,244},{4,243},{5,246},{6,245},{7,248},{8... | collective-permute-start | bytes 393224 | tf_op jit(solution)/shard_map/ppermute | solution.py:579
